TPU v7x, 512 devices: a whole 4x8x8 slice. The times are simulated.
512 devices in a mesh: tm: 128 (over z, y, core), swath: 4 (over x).
Axes of the slice: x: 4, y: 8, z: 8, core: 2. Of those that a mesh axis runs over, the one named last changes fastest.
Arguments:
- design: bfloat16 [128, 2048, 512], P('tm', 'swath'), may hold values from -6 to 6
- process: bfloat16 [128, 512, 512], P('tm', 'swath')
- prior_prec: float32 [128, 512], P('tm', 'swath'), may hold values from 0.05 to 0.5
- routes: int32 [128, 16], P('tm', 'swath'), may hold values from -1 to 127, as said below
- counts: int32 [128, 4], P('tm', 'swath'), may hold values from 1 to 4
Outputs:
- reduced_diag: float32 [128, 512, 512], P('tm', 'swath')
- reduced_coupling: float32 [128, 512, 512], P('tm', 'swath')
Inputs may be any that keep to these rules, and one draw needn't show every extreme that they name: `routes`: each value is the holder's own time block i or i + 1, or -1 only where i + 1 would be 128; of one holder's 4 blocks, exactly 2 name i and the others i + 1 or -1.
All inputs are finite; a program needn't handle non-finite values.
Results may differ from a plain program's by a relative error of at most 0.00073.
Values may be sent and summed in bfloat16 or wider, within the bound.
No kernel may reach another device: no remote copies, remote signals or barrier semaphores. Data moves between devices by JAX's collectives and lax.ppermute only.
A program may use at most 64 MiB of HBM per device.

v0:
```python
import jax
import jax.numpy as jnp
from jax import lax
from jax.sharding import PartitionSpec as P

LEVELS = 3


def passed_along(block, axis, distance):
    devices = range(lax.axis_size(axis))
    route = [(i - distance, i) for i in devices if i - distance in devices]
    return lax.ppermute(block, axis, route)


def tri_solve(factor, right):
    return lax.linalg.triangular_solve(factor, right, left_side=True, lower=True)


def inner_rows(left_side, right_side):
    return lax.dot_general(
        left_side,
        right_side,
        (((0,), (0,)), ((), ())),
        precision=lax.Precision.HIGHEST,
        preferred_element_type=jnp.float32,
    )


def compact(scaled, wanted, slot_count):
    sort_key = jnp.where(wanted, 0, 1).astype(jnp.int32)
    picked = jnp.argsort(sort_key, stable=True)[:slot_count]
    kept = jnp.take(sort_key, picked) == 0
    return jnp.where(kept[:, None, None], scaled[picked], 0.0).astype(jnp.bfloat16)


def shards(design, process, prior_prec, routes, counts):
    row_count = process.shape[1]
    order_size = process.shape[2]
    time_count = lax.axis_size("tm")
    my_time = lax.axis_index("tm")
    swath_index = lax.axis_index("swath")
    block_count = routes.shape[1]
    slot_count = block_count // 2
    block_rows = design.shape[1] // block_count
    total_slots = 2 * slot_count * block_rows * lax.axis_size("swath")
    row_start = swath_index * row_count
    raw_rows = design[0].reshape(block_count, block_rows, order_size).astype(jnp.float32)
    mean_sq = jnp.mean(raw_rows * raw_rows, axis=-1, keepdims=True)
    scaled = raw_rows * lax.rsqrt(4.0 * total_slots * (mean_sq + 1e-06))
    live = jnp.arange(block_count) < counts[0, 0]
    target = routes[0]
    own_blocks = compact(scaled, live & (target == my_time), slot_count)
    ahead_blocks = compact(scaled, live & (target == my_time + 1), slot_count)
    incoming, previous = passed_along((ahead_blocks, process), "tm", 1)
    gram_input = jnp.concatenate([own_blocks, incoming], axis=0).reshape(-1, order_size)
    shard_rows = lax.all_gather(gram_input, "swath", axis=0, tiled=True)
    columns = lax.dynamic_slice_in_dim(shard_rows, row_start, row_count, 1)
    gram = lax.dot_general(
        columns, shard_rows, (((0,), (0,)), ((), ())), preferred_element_type=jnp.float32
    )
    unit_rows = jnp.arange(order_size)[None, :] == jnp.arange(row_count)[:, None] + row_start
    diag_rows = previous[0].astype(jnp.float32) + process[0].astype(jnp.float32) + gram
    diag_rows = diag_rows + jnp.where(unit_rows, prior_prec[0][:, None], 0.0)
    coup_rows = -process[0].astype(jnp.float32)
    unit_full = jnp.eye(order_size, dtype=jnp.float32)
    for level in range(LEVELS):
        distance = 2**level
        full_diag, full_coup = (
            lax.all_gather(diag_rows, "swath", axis=0, tiled=True),
            lax.all_gather(coup_rows, "swath", axis=0, tiled=True),
        )
        factor = jnp.linalg.cholesky(full_diag)
        solved = tri_solve(factor, full_coup)
        own_cols = lax.dynamic_slice_in_dim(solved, row_start, row_count, 1)
        eliminated = inner_rows(own_cols, solved)
        left_term = passed_along(eliminated, "tm", distance)
        far_factor, far_solved = passed_along((factor, solved), "tm", -distance)
        has_partner = my_time + distance < time_count
        far_factor = jnp.where(has_partner, far_factor, unit_full)
        cross = tri_solve(far_factor, full_coup.T)
        cross_cols = lax.dynamic_slice_in_dim(cross, row_start, row_count, 1)
        right_term = inner_rows(cross_cols, cross)
        new_coupling = inner_rows(cross_cols, far_solved)
        diag_rows = diag_rows - left_term - jnp.where(has_partner, right_term, 0.0)
        coup_rows = -new_coupling
    return (diag_rows[None], coup_rows[None])


def solution(mesh):
    return jax.shard_map(
        shards,
        mesh=mesh,
        in_specs=(
            P("tm", "swath", None),
            P("tm", "swath", None),
            P("tm", "swath"),
            P("tm", "swath"),
            P("tm", "swath"),
        ),
        out_specs=(P("tm", "swath", None), P("tm", "swath", None)),
        check_vma=False,
    )
```

profile of v0, /device:TPU:16, one launch (start us, length us, event | category | flops | bytes accessed | tf_op | source)
XLA Modules:
  0.0 882.1 jit_solution(11233047935860242572)
XLA Ops:
  28.9 35.5 %all-gather.9.cloned.1.call-done = bf16[2048,512]{1,0:T(8,128)(2,1)} async-done(((bf16[512,512]{1,0:T(8,128)(2,1)}), bf16[2048,512]{1,0:T(8,128)(2,1)}) %all-gather.9.cloned.1.call-update) | async-done | bytes 2097168 | tf_op jit(solution)/shard_map/all_gather | solution.py:56
  68.6 30.6 %all-gather.11.cloned.1.call-done = f32[512,512]{0,1:T(8,128)} async-done(((f32[128,512]{0,1:T(8,128)}), f32[512,512]{0,1:T(8,128)}) %all-gather.11.cloned.1.call-update) | async-done | bytes 1048592 | tf_op jit(solution)/shard_map/all_gather | solution.py:69
  101.1 11.7 %cholesky.374 = f32[128,128]{1,0:T(8,128)S(1)} custom-call(f32[128,128]{1,0:T(8,128)S(1)} %cholesky.586), custom_call_target="Cholesky" | custom-call | tf_op jit(solution)/shard_map/jit(cholesky)/cholesky | solution.py:72
  123.5 11.7 %cholesky.393 = f32[128,128]{1,0:T(8,128)S(1)} custom-call(f32[128,128]{1,0:T(8,128)S(1)} %cholesky.590), custom_call_target="Cholesky" | custom-call | tf_op jit(solution)/shard_map/jit(cholesky)/cholesky | solution.py:72
  146.1 11.7 %cholesky.414 = f32[128,128]{1,0:T(8,128)S(1)} custom-call(f32[128,128]{1,0:T(8,128)S(1)} %cholesky.595), custom_call_target="Cholesky" | custom-call | tf_op jit(solution)/shard_map/jit(cholesky)/cholesky | solution.py:72
  168.3 11.7 %cholesky.431 = f32[128,128]{1,0:T(8,128)S(1)} custom-call(f32[128,128]{1,0:T(8,128)S(1)} %convolution_subtract_fusion.14), custom_call_target="Cholesky" | custom-call | tf_op jit(solution)/shard_map/jit(cholesky)/cholesky | solution.py:72
  193.0 39.3 %custom-call.37 = f32[4,128,128]{1,2,0:T(8,128)S(1)} custom-call(f32[4,128,128]{2,1,0:T(8,128)S(1)} %get-tuple-element.47), custom_call_target="InvertDiagBlocksLowerTriangular" | custom-call | tf_op jit(solution)/shard_map/triangular_solve/custom-call.3 | solution.py:16
  262.2 40.7 %custom-call.38 = f32[4,128,128]{1,2,0:T(8,128)} custom-call(f32[4,128,128]{2,1,0:T(8,128)} %get-tuple-element.48), custom_call_target="InvertDiagBlocksLowerTriangular" | custom-call | tf_op jit(solution)/shard_map/triangular_solve/custom-call.3 | solution.py:16
  314.4 12.3 %collective-permute-done.4 = f32[512,512]{1,0:T(8,128)S(1)} collective-permute-done((f32[512,512]{1,0:T(8,128)S(1)}, f32[512,512]{1,0:T(8,128)S(1)}, u32[]{:S(2)}, u32[]{:S(2)}) %collective-permute-start.4) | collective-permute-done | bytes 1048608 | tf_op jit(solution)/shard_map/ppermute | solution.py:12
  328.6 15.1 %all-gather.13.cloned.1.call-done = f32[512,512]{0,1:T(8,128)} async-done(((f32[128,512]{0,1:T(8,128)}), f32[512,512]{0,1:T(8,128)}) %all-gather.13.cloned.1.call-update) | async-done | bytes 1048592 | tf_op jit(solution)/shard_map/all_gather | solution.py:69
  345.6 11.7 %cholesky.446 = f32[128,128]{1,0:T(8,128)S(1)} custom-call(f32[128,128]{1,0:T(8,128)S(1)} %cholesky.599), custom_call_target="Cholesky" | custom-call | tf_op jit(solution)/shard_map/jit(cholesky)/cholesky | solution.py:72
  368.0 11.7 %cholesky.465 = f32[128,128]{1,0:T(8,128)S(1)} custom-call(f32[128,128]{1,0:T(8,128)S(1)} %cholesky.603), custom_call_target="Cholesky" | custom-call | tf_op jit(solution)/shard_map/jit(cholesky)/cholesky | solution.py:72
  390.4 11.7 %cholesky.486 = f32[128,128]{1,0:T(8,128)S(1)} custom-call(f32[128,128]{1,0:T(8,128)S(1)} %cholesky.608), custom_call_target="Cholesky" | custom-call | tf_op jit(solution)/shard_map/jit(cholesky)/cholesky | solution.py:72
  412.5 11.7 %cholesky.503 = f32[128,128]{1,0:T(8,128)S(1)} custom-call(f32[128,128]{1,0:T(8,128)S(1)} %convolution_subtract_fusion.13), custom_call_target="Cholesky" | custom-call | tf_op jit(solution)/shard_map/jit(cholesky)/cholesky | solution.py:72
  437.3 39.3 %custom-call.42 = f32[4,128,128]{1,2,0:T(8,128)S(1)} custom-call(f32[4,128,128]{2,1,0:T(8,128)S(1)} %get-tuple-element.49), custom_call_target="InvertDiagBlocksLowerTriangular" | custom-call | tf_op jit(solution)/shard_map/triangular_solve/custom-call.3 | solution.py:16
  490.7 15.6 %collective-permute-done.6 = f32[512,512]{1,0:T(8,128)S(1)} collective-permute-done((f32[512,512]{1,0:T(8,128)S(1)}, f32[512,512]{1,0:T(8,128)S(1)}, u32[]{:S(2)}, u32[]{:S(2)}) %collective-permute-start.6) | collective-permute-done | bytes 1048608 | tf_op jit(solution)/shard_map/ppermute | solution.py:12
  517.3 40.7 %custom-call.43 = f32[4,128,128]{1,2,0:T(8,128)} custom-call(f32[4,128,128]{2,1,0:T(8,128)} %get-tuple-element.50), custom_call_target="InvertDiagBlocksLowerTriangular" | custom-call | tf_op jit(solution)/shard_map/triangular_solve/custom-call.3 | solution.py:16
  570.0 23.3 %collective-permute-done.7 = f32[512,512]{1,0:T(8,128)S(1)} collective-permute-done((f32[512,512]{1,0:T(8,128)S(1)}, f32[512,512]{1,0:T(8,128)S(1)}, u32[]{:S(2)}, u32[]{:S(2)}) %collective-permute-start.7) | collective-permute-done | bytes 1048608 | tf_op jit(solution)/shard_map/ppermute | solution.py:12
  601.6 11.7 %cholesky.518 = f32[128,128]{1,0:T(8,128)S(1)} custom-call(f32[128,128]{1,0:T(8,128)S(1)} %cholesky.612), custom_call_target="Cholesky" | custom-call | tf_op jit(solution)/shard_map/jit(cholesky)/cholesky | solution.py:72
  624.0 11.7 %cholesky.537 = f32[128,128]{1,0:T(8,128)S(1)} custom-call(f32[128,128]{1,0:T(8,128)S(1)} %cholesky.616), custom_call_target="Cholesky" | custom-call | tf_op jit(solution)/shard_map/jit(cholesky)/cholesky | solution.py:72
  668.6 12.1 %cholesky.575 = f32[128,128]{1,0:T(8,128)S(1)} custom-call(f32[128,128]{1,0:T(8,128)S(1)} %convolution_subtract_fusion.12), custom_call_target="Cholesky" | custom-call | tf_op jit(solution)/shard_map/jit(cholesky)/cholesky | solution.py:72
  693.9 39.3 %custom-call.47 = f32[4,128,128]{1,2,0:T(8,128)S(1)} custom-call(f32[4,128,128]{2,1,0:T(8,128)S(1)} %get-tuple-element.51), custom_call_target="InvertDiagBlocksLowerTriangular" | custom-call | tf_op jit(solution)/shard_map/triangular_solve/custom-call.3 | solution.py:16
  751.6 59.3 %collective-permute-done.9 = f32[512,512]{1,0:T(8,128)S(1)} collective-permute-done((f32[512,512]{1,0:T(8,128)S(1)}, f32[512,512]{1,0:T(8,128)S(1)}, u32[]{:S(2)}, u32[]{:S(2)}) %collective-permute-start.9) | collective-permute-done | bytes 1048608 | tf_op jit(solution)/shard_map/ppermute | solution.py:12
  822.2 40.7 %custom-call.48 = f32[4,128,128]{1,2,0:T(8,128)} custom-call(f32[4,128,128]{2,1,0:T(8,128)} %get-tuple-element.52), custom_call_target="InvertDiagBlocksLowerTriangular" | custom-call | tf_op jit(solution)/shard_map/triangular_solve/custom-call.3 | solution.py:16
  (308 shorter events, 351.0 us)
Async XLA Ops:
  7.2 57.3 %all-gather.9.cloned.1.call-start = ((), (), s32[]{:S(2)}) async-start(), calls=%async_computation | async-start | bytes 2621440 | tf_op jit(solution)/shard_map/all_gather | solution.py:56
  13.1 9.3 %copy-start.12 = (bf16[1,128,512]{2,1,0:T(8,128)(2,1)S(1)}, bf16[1,128,512]{2,1,0:T(8,128)(2,1)}, u32[]{:S(2)}) copy-start(bf16[1,128,512]{2,1,0:T(8,128)(2,1)} %param.11) | copy-start | bytes 393220
  13.7 50.7 %copy-start.13 = (f32[1,128]{1,0:T(1,128)S(1)}, f32[1,128]{1,0:T(1,128)}, u32[]{:S(2)}) copy-start(f32[1,128]{1,0:T(1,128)} %param.12) | copy-start | bytes 1540
  13.9 7.7 collective-permute-start.1
  22.4 76.8 %all-gather.11.cloned.1.call-start = ((), (), s32[]{:S(2)}) async-start(), calls=%async_computation.1 | async-start | bytes 1310720 | tf_op jit(solution)/shard_map/all_gather | solution.py:69
  22.6 6.3 collective-permute-start
  67.8 164.6 %all-gather.21.cloned.1.call-start = ((), (), s32[]{:S(2)}) async-start(), calls=%async_computation.6 | async-start | bytes 1310720 | tf_op jit(solution)/shard_map/all_gather | solution.py:70
  68.6 275.1 %all-gather.13.cloned.1.call-start = ((), (), s32[]{:S(2)}) async-start(), calls=%async_computation.2 | async-start | bytes 1310720 | tf_op jit(solution)/shard_map/all_gather | solution.py:69
  236.9 14.2 %collective-permute-start.3 = (f32[512,512]{1,0:T(8,128)S(1)}, f32[512,512]{1,0:T(8,128)S(1)}, u32[]{:S(2)}, u32[]{:S(2)}) collective-permute-start(f32[512,512]{1,0:T(8,128)S(1)} %get-tuple-element.110), channel_id=1, source_target_pairs={{4,0},{8,4},{12,8},{16,12},{20,16},{24,20},{28,24},{32,28},{36,32}... | collective-permute-start | bytes 3145736 | tf_op jit(solution)/shard_map/ppermute | solution.py:12
  243.7 64.2 %collective-permute-start.2 = (f32[128,512]{0,1:T(8,128)}, f32[128,512]{0,1:T(8,128)S(1)}, u32[]{:S(2)}, u32[]{:S(2)}) collective-permute-start(f32[128,512]{0,1:T(8,128)} %fusion.103), channel_id=1, source_target_pairs={{0,4},{4,8},{8,12},{12,16},{16,20},{20,24},{24,28},{28,32},{32,36}... | collective-permute-start | bytes 786440 | tf_op jit(solution)/shard_map/ppermute | solution.py:12
  310.5 166.1 %all-gather.15.cloned.1.call-start = ((), (), s32[]{:S(2)}) async-start(), calls=%async_computation.3 | async-start | bytes 1310720 | tf_op jit(solution)/shard_map/all_gather | solution.py:70
  310.6 16.1 %collective-permute-start.4 = (f32[512,512]{1,0:T(8,128)S(1)}, f32[512,512]{1,0:T(8,128)S(1)}, u32[]{:S(2)}, u32[]{:S(2)}) collective-permute-start(f32[512,512]{1,0:T(8,128)S(1)} %pad_maximum_fusion), channel_id=1, source_target_pairs={{4,0},{8,4},{12,8},{16,12},{20,16},{24,20},{28,24},{32,28},{36,32}... | collective-permute-start | bytes 3145736 | tf_op jit(solution)/shard_map/ppermute | solution.py:12
  328.2 271.6 %all-gather.17.cloned.1.call-start = ((), (), s32[]{:S(2)}) async-start(), calls=%async_computation.4 | async-start | bytes 1310720 | tf_op jit(solution)/shard_map/all_gather | solution.py:69
  476.6 6.1 copy-start.1
  480.3 25.9 %collective-permute-start.6 = (f32[512,512]{1,0:T(8,128)S(1)}, f32[512,512]{1,0:T(8,128)S(1)}, u32[]{:S(2)}, u32[]{:S(2)}) collective-permute-start(f32[512,512]{1,0:T(8,128)S(1)} %get-tuple-element.108), channel_id=1, source_target_pairs={{8,0},{12,4},{16,8},{20,12},{24,16},{28,20},{32,24},{36,28},{40,32... | collective-permute-start | bytes 3145736 | tf_op jit(solution)/shard_map/ppermute | solution.py:12
  486.9 77.9 %collective-permute-start.5 = (f32[128,512]{0,1:T(8,128)}, f32[128,512]{0,1:T(8,128)S(1)}, u32[]{:S(2)}, u32[]{:S(2)}) collective-permute-start(f32[128,512]{0,1:T(8,128)} %fusion.101), channel_id=1, source_target_pairs={{0,8},{4,12},{8,16},{12,20},{16,24},{20,28},{24,32},{28,36},{32,40... | collective-permute-start | bytes 786440 | tf_op jit(solution)/shard_map/ppermute | solution.py:12
  558.1 4.2 copy-start.10
  567.3 165.9 %all-gather.19.cloned.1.call-start = ((), (), s32[]{:S(2)}) async-start(), calls=%async_computation.5 | async-start | bytes 1310720 | tf_op jit(solution)/shard_map/all_gather | solution.py:70
  567.4 26.0 %collective-permute-start.7 = (f32[512,512]{1,0:T(8,128)S(1)}, f32[512,512]{1,0:T(8,128)S(1)}, u32[]{:S(2)}, u32[]{:S(2)}) collective-permute-start(f32[512,512]{1,0:T(8,128)S(1)} %pad_maximum_fusion.2), channel_id=1, source_target_pairs={{8,0},{12,4},{16,8},{20,12},{24,16},{28,20},{32,24},{36,28},{40,32... | collective-permute-start | bytes 3145736 | tf_op jit(solution)/shard_map/ppermute | solution.py:12
  733.2 6.1 copy-start
  736.9 74.0 %collective-permute-start.9 = (f32[512,512]{1,0:T(8,128)S(1)}, f32[512,512]{1,0:T(8,128)S(1)}, u32[]{:S(2)}, u32[]{:S(2)}) collective-permute-start(f32[512,512]{1,0:T(8,128)S(1)} %get-tuple-element.106), channel_id=1, source_target_pairs={{16,0},{20,4},{24,8},{28,12},{32,16},{36,20},{40,24},{44,28},{48,3... | collective-permute-start | bytes 3145736 | tf_op jit(solution)/shard_map/ppermute | solution.py:12
  740.9 131.4 %collective-permute-start.10 = (f32[512,512]{1,0:T(8,128)S(1)}, f32[512,512]{1,0:T(8,128)}, u32[]{:S(2)}, u32[]{:S(2)}) collective-permute-start(f32[512,512]{1,0:T(8,128)S(1)} %pad_maximum_fusion.4), channel_id=1, source_target_pairs={{16,0},{20,4},{24,8},{28,12},{32,16},{36,20},{40,24},{44,28},{48,3... | collective-permute-start | bytes 3145736 | tf_op jit(solution)/shard_map/ppermute | solution.py:12
  745.4 124.3 %collective-permute-start.8 = (f32[128,512]{0,1:T(8,128)}, f32[128,512]{0,1:T(8,128)S(1)}, u32[]{:S(2)}, u32[]{:S(2)}) collective-permute-start(f32[128,512]{0,1:T(8,128)} %fusion.99), channel_id=1, source_target_pairs={{0,16},{4,20},{8,24},{12,28},{16,32},{20,36},{24,40},{28,44},{32,4... | collective-permute-start | bytes 786440 | tf_op jit(solution)/shard_map/ppermute | solution.py:12
  862.9 4.2 copy-start.11
  (8 other events, 17.1 us)
Sparse Core Ops, SparseCore 0:
  22.5 41.8 all-gather.8
  67.9 31.2 all-gather.10
  101.9 32.4 all-gather.20
  310.6 33.0 all-gather.12
  346.2 30.5 all-gather.14
  567.5 32.2 all-gather.16
  602.4 30.6 all-gather.18
where the time goes:
time: 894 us; the launch traced here: 882 us
  other arithmetic  487 us (54%)
  waiting for transfers between devices  210 us (23%)
  local copies, waits for them, and re-layouts  64.4 us (7%)
  matrix products  64 us (7%)
  starting transfers between devices  32.1 us (4%)
  between operations  23.4 us (3%)
    another operation x19, other arithmetic, tri_solve(): lax.linalg.triangular_solve(factor, right, left_side=True, lower=True)  242 us
    another operation x45, other arithmetic, shards(): factor = jnp.linalg.cholesky(full_diag)  238 us
    ppermute x11, waiting for transfers between devices, passed_along(): return lax.ppermute(block, axis, route)  124 us
    another operation x79, local copies, waits for them, and re-layouts, tri_solve(): lax.linalg.triangular_solve(factor, right, left_side=True, lower=True)  55.7 us
    all_gather x3, waiting for transfers between devices, shards(): lax.all_gather(diag_rows, 'swath', axis=0, tiled=True)  50.5 us
    all_gather x1, waiting for transfers between devices, shards(): shard_rows = lax.all_gather(gram_input, 'swath', axis=0, tiled=True)  35.5 us
    another operation x42, matrix products, tri_solve(): lax.linalg.triangular_solve(factor, right, left_side=True, lower=True)  35 us
    ppermute x11, starting transfers between devices, passed_along(): return lax.ppermute(block, axis, route)  31.4 us
  transfers between devices with their start and end apart: 18, of which 11 were waited for; matrix products, arithmetic and copies ran while one was open for 66% of the time, Pallas kernels for 0%

commit v1 on v0

--- a/solution.py
+++ b/solution.py
@@ -66,7 +66,12 @@
     for level in range(LEVELS):
         distance = 2**level
         full_diag, full_coup = (
-            lax.all_gather(diag_rows, "swath", axis=0, tiled=True),
+            jnp.concatenate(
+                lax.all_to_all(
+                    jnp.stack([diag_rows] * lax.axis_size("swath"), axis=0), "swath", 0, 0
+                ),
+                axis=0,
+            ),
             lax.all_gather(coup_rows, "swath", axis=0, tiled=True),
         )
         factor = jnp.linalg.cholesky(full_diag)

time: 894 us -> 820 us (0.917)
  the two profiles are of different devices: /device:TPU:16 before, /device:TPU:57 now
where the time goes in v1:
time: 820 us; the launch traced here: 809 us
  other arithmetic  490 us (60%)
  waiting for transfers between devices  124 us (15%)
  local copies, waits for them, and re-layouts  59 us (7%)
  matrix products  57.8 us (7%)
  starting transfers between devices  53.5 us (7%)
  between operations  23.5 us (3%)
    another operation x19, other arithmetic, tri_solve(): lax.linalg.triangular_solve(factor, right, left_side=True, lower=True)  244 us
    another operation x45, other arithmetic, shards(): factor = jnp.linalg.cholesky(full_diag)  239 us
    ppermute x11, waiting for transfers between devices, passed_along(): return lax.ppermute(block, axis, route)  54.9 us
    another operation x79, local copies, waits for them, and re-layouts, tri_solve(): lax.linalg.triangular_solve(factor, right, left_side=True, lower=True)  51 us
    ppermute x11, starting transfers between devices, passed_along(): return lax.ppermute(block, axis, route)  42.2 us
    all_to_all x3, waiting for transfers between devices, shards(): lax.all_to_all(jnp.stack([diag_rows] * lax.axis_size('swath'), axis=0), '...  35.6 us
    another operation x42, matrix products, tri_solve(): lax.linalg.triangular_solve(factor, right, left_side=True, lower=True)  34.1 us
    all_gather x1, waiting for transfers between devices, shards(): shard_rows = lax.all_gather(gram_input, 'swath', axis=0, tiled=True)  33.7 us
  transfers between devices with their start and end apart: 18, of which 10 were waited for; matrix products, arithmetic and copies ran while one was open for 72% of the time, Pallas kernels for 0%

profile of v1, /device:TPU:57, one launch (start us, length us, event | category | flops | bytes accessed | tf_op | source)
XLA Modules:
  0.0 808.5 jit_solution(2160679278824384987)
XLA Ops:
  30.2 33.7 %all-gather.6.cloned.1.call-done = bf16[2048,512]{1,0:T(8,128)(2,1)} async-done(((bf16[512,512]{1,0:T(8,128)(2,1)}), bf16[2048,512]{1,0:T(8,128)(2,1)}) %all-gather.6.cloned.1.call-update) | async-done | bytes 2097168 | tf_op jit(solution)/shard_map/all_gather | solution.py:56
  71.8 13.6 %all-to-all-done = f32[4,128,512]{1,2,0:T(8,128)S(1)} async-done(((f32[4,128,512]{1,2,0:T(8,128)}), f32[4,128,512]{1,2,0:T(8,128)S(1)}, u32[]{:S(2)}, u32[]{:S(2)}) %all-to-all-start) | async-done | bytes 1048608 | tf_op jit(solution)/shard_map/all_to_all | solution.py:70
  86.1 11.7 %cholesky.374 = f32[128,128]{1,0:T(8,128)S(1)} custom-call(f32[128,128]{1,0:T(8,128)S(1)} %cholesky.586), custom_call_target="Cholesky" | custom-call | tf_op jit(solution)/shard_map/jit(cholesky)/cholesky | solution.py:77
  108.5 11.7 %cholesky.393 = f32[128,128]{1,0:T(8,128)S(1)} custom-call(f32[128,128]{1,0:T(8,128)S(1)} %cholesky.590), custom_call_target="Cholesky" | custom-call | tf_op jit(solution)/shard_map/jit(cholesky)/cholesky | solution.py:77
  131.2 11.7 %cholesky.414 = f32[128,128]{1,0:T(8,128)S(1)} custom-call(f32[128,128]{1,0:T(8,128)S(1)} %cholesky.595), custom_call_target="Cholesky" | custom-call | tf_op jit(solution)/shard_map/jit(cholesky)/cholesky | solution.py:77
  153.3 11.7 %cholesky.431 = f32[128,128]{1,0:T(8,128)S(1)} custom-call(f32[128,128]{1,0:T(8,128)S(1)} %convolution_subtract_fusion.14), custom_call_target="Cholesky" | custom-call | tf_op jit(solution)/shard_map/jit(cholesky)/cholesky | solution.py:77
  178.9 39.9 %custom-call.37 = f32[4,128,128]{1,2,0:T(8,128)} custom-call(f32[4,128,128]{2,1,0:T(8,128)S(1)} %get-tuple-element.47), custom_call_target="InvertDiagBlocksLowerTriangular" | custom-call | tf_op jit(solution)/shard_map/triangular_solve/custom-call.3 | solution.py:16
  242.5 10.4 %while.13 = (s32[]{:T(128)}, f32[512,512]{1,0:T(8,128)S(1)}, s32[4,2]{0,1:T(2,128)S(1)}, f32[4,128,128]{2,1,0:T(8,128)}, s32[]{:T(128)}) while((s32[]{:T(128)}, f32[512,512]{1,0:T(8,128)S(1)}, s32[4,2]{0,1:T(2,128)S(1)}, f32[4,128,128]{2,1,0:T(8,128)}, s32[]{:T(128)}) %tuple.149), condition=%wide.while_cond.clone, body=%wide.while_body.clone.sunk | while | flops 2 | bytes 132205 | solution.py:16
  252.9 40.7 %custom-call.38 = f32[4,128,128]{1,2,0:T(8,128)} custom-call(f32[4,128,128]{2,1,0:T(8,128)} %get-tuple-element.48), custom_call_target="InvertDiagBlocksLowerTriangular" | custom-call | tf_op jit(solution)/shard_map/triangular_solve/custom-call.3 | solution.py:16
  320.9 11.7 %cholesky.446 = f32[128,128]{1,0:T(8,128)S(1)} custom-call(f32[128,128]{1,0:T(8,128)S(1)} %cholesky.599), custom_call_target="Cholesky" | custom-call | tf_op jit(solution)/shard_map/jit(cholesky)/cholesky | solution.py:77
  343.2 11.7 %cholesky.465 = f32[128,128]{1,0:T(8,128)S(1)} custom-call(f32[128,128]{1,0:T(8,128)S(1)} %cholesky.603), custom_call_target="Cholesky" | custom-call | tf_op jit(solution)/shard_map/jit(cholesky)/cholesky | solution.py:77
  365.6 11.7 %cholesky.486 = f32[128,128]{1,0:T(8,128)S(1)} custom-call(f32[128,128]{1,0:T(8,128)S(1)} %cholesky.608), custom_call_target="Cholesky" | custom-call | tf_op jit(solution)/shard_map/jit(cholesky)/cholesky | solution.py:77
  387.8 12.1 %cholesky.503 = f32[128,128]{1,0:T(8,128)S(1)} custom-call(f32[128,128]{1,0:T(8,128)S(1)} %convolution_subtract_fusion.13), custom_call_target="Cholesky" | custom-call | tf_op jit(solution)/shard_map/jit(cholesky)/cholesky | solution.py:77
  414.3 39.3 %custom-call.42 = f32[4,128,128]{1,2,0:T(8,128)S(1)} custom-call(f32[4,128,128]{2,1,0:T(8,128)S(1)} %get-tuple-element.49), custom_call_target="InvertDiagBlocksLowerTriangular" | custom-call | tf_op jit(solution)/shard_map/triangular_solve/custom-call.3 | solution.py:16
  471.0 12.1 %collective-permute-done.6 = f32[512,512]{1,0:T(8,128)} collective-permute-done((f32[512,512]{1,0:T(8,128)}, f32[512,512]{1,0:T(8,128)}, u32[]{:S(2)}, u32[]{:S(2)}) %collective-permute-start.6) | collective-permute-done | bytes 1048608 | tf_op jit(solution)/shard_map/ppermute | solution.py:12
  492.7 39.9 %custom-call.43 = f32[4,128,128]{1,2,0:T(8,128)} custom-call(f32[4,128,128]{2,1,0:T(8,128)S(1)} %get-tuple-element.50), custom_call_target="InvertDiagBlocksLowerTriangular" | custom-call | tf_op jit(solution)/shard_map/triangular_solve/custom-call.3 | solution.py:16
  548.9 11.9 %all-to-all-done.2 = f32[4,128,512]{1,2,0:T(8,128)S(1)} async-done(((f32[4,128,512]{1,2,0:T(8,128)}), f32[4,128,512]{1,2,0:T(8,128)S(1)}, u32[]{:S(2)}, u32[]{:S(2)}) %all-to-all-start.2) | async-done | bytes 1048608 | tf_op jit(solution)/shard_map/all_to_all | solution.py:70
  561.4 11.7 %cholesky.518 = f32[128,128]{1,0:T(8,128)S(1)} custom-call(f32[128,128]{1,0:T(8,128)S(1)} %cholesky.612), custom_call_target="Cholesky" | custom-call | tf_op jit(solution)/shard_map/jit(cholesky)/cholesky | solution.py:77
  583.7 11.7 %cholesky.537 = f32[128,128]{1,0:T(8,128)S(1)} custom-call(f32[128,128]{1,0:T(8,128)S(1)} %cholesky.616), custom_call_target="Cholesky" | custom-call | tf_op jit(solution)/shard_map/jit(cholesky)/cholesky | solution.py:77
  606.2 11.7 %cholesky.558 = f32[128,128]{1,0:T(8,128)S(1)} custom-call(f32[128,128]{1,0:T(8,128)S(1)} %cholesky.621), custom_call_target="Cholesky" | custom-call | tf_op jit(solution)/shard_map/jit(cholesky)/cholesky | solution.py:77
  628.3 12.1 %cholesky.575 = f32[128,128]{1,0:T(8,128)S(1)} custom-call(f32[128,128]{1,0:T(8,128)S(1)} %convolution_subtract_fusion.12), custom_call_target="Cholesky" | custom-call | tf_op jit(solution)/shard_map/jit(cholesky)/cholesky | solution.py:77
  656.9 39.9 %custom-call.47 = f32[4,128,128]{1,2,0:T(8,128)} custom-call(f32[4,128,128]{2,1,0:T(8,128)S(1)} %get-tuple-element.51), custom_call_target="InvertDiagBlocksLowerTriangular" | custom-call | tf_op jit(solution)/shard_map/triangular_solve/custom-call.3 | solution.py:16
  705.1 39.3 %custom-call.48 = f32[4,128,128]{1,2,0:T(8,128)S(1)} custom-call(f32[4,128,128]{2,1,0:T(8,128)S(1)} %get-tuple-element.52), custom_call_target="InvertDiagBlocksLowerTriangular" | custom-call | tf_op jit(solution)/shard_map/triangular_solve/custom-call.3 | solution.py:16
  770.6 29.7 %collective-permute-done.10 = f32[512,512]{1,0:T(8,128)S(1)} collective-permute-done((f32[512,512]{1,0:T(8,128)S(1)}, f32[512,512]{1,0:T(8,128)S(1)}, u32[]{:S(2)}, u32[]{:S(2)}) %collective-permute-start.10) | collective-permute-done | bytes 1048608 | tf_op jit(solution)/shard_map/ppermute | solution.py:12
  (306 shorter events, 343.2 us)
Async XLA Ops:
  7.2 56.8 %all-gather.6.cloned.1.call-start = ((), (), s32[]{:S(2)}) async-start(), calls=%async_computation.3 | async-start | bytes 2621440 | tf_op jit(solution)/shard_map/all_gather | solution.py:56
  13.1 8.7 %copy-start.5 = (bf16[1,128,512]{2,1,0:T(8,128)(2,1)S(1)}, bf16[1,128,512]{2,1,0:T(8,128)(2,1)}, u32[]{:S(2)}) copy-start(bf16[1,128,512]{2,1,0:T(8,128)(2,1)} %param.11) | copy-start | bytes 393220
  13.2 50.8 %copy-start.10 = (f32[1,128]{1,0:T(1,128)S(1)}, f32[1,128]{1,0:T(1,128)}, u32[]{:S(2)}) copy-start(f32[1,128]{1,0:T(1,128)} %param.12) | copy-start | bytes 1540
  13.9 7.1 collective-permute-start.1
  21.8 8.4 %collective-permute-start = (bf16[1,128,512]{2,1,0:T(8,128)(2,1)S(1)}, bf16[1,128,512]{2,1,0:T(8,128)(2,1)S(1)}, u32[]{:S(2)}, u32[]{:S(2)}) collective-permute-start(bf16[1,128,512]{2,1,0:T(8,128)(2,1)S(1)} %copy-done.5), channel_id=1, source_target_pairs={{0,4},{4,8},{8,12},{12,16},{16,20},{20,24},{24,28},{28,32},{32,36}... | collective-permute-start | bytes 393224 | tf_op jit(solution)/shard_map/ppermute | solution.py:12
  67.5 18.0 %all-to-all-start = ((f32[4,128,512]{1,2,0:T(8,128)}), f32[4,128,512]{1,2,0:T(8,128)S(1)}, u32[]{:S(2)}, u32[]{:S(2)}) async-start(f32[4,128,512]{1,2,0:T(8,128)} %stack.6), calls=%async_computation | async-start | bytes 2097152 | tf_op jit(solution)/shard_map/all_to_all | solution.py:70
  71.0 147.9 %all-gather.12.cloned.1.call-start = ((), (), s32[]{:S(2)}) async-start(), calls=%async_computation.6 | async-start | bytes 1310720 | tf_op jit(solution)/shard_map/all_gather | solution.py:75
  218.9 8.0 copy-start.6
  223.4 18.2 %collective-permute-start.3 = (f32[512,512]{1,0:T(8,128)S(1)}, f32[512,512]{1,0:T(8,128)S(1)}, u32[]{:S(2)}, u32[]{:S(2)}) collective-permute-start(f32[512,512]{1,0:T(8,128)S(1)} %get-tuple-element.106), channel_id=1, source_target_pairs={{4,0},{8,4},{12,8},{16,12},{20,16},{24,20},{28,24},{32,28},{36,32}... | collective-permute-start | bytes 3145736 | tf_op jit(solution)/shard_map/ppermute | solution.py:12
  228.5 78.9 %collective-permute-start.4 = (f32[512,512]{1,0:T(8,128)S(1)}, f32[512,512]{1,0:T(8,128)}, u32[]{:S(2)}, u32[]{:S(2)}) collective-permute-start(f32[512,512]{1,0:T(8,128)S(1)} %pad_maximum_fusion), channel_id=1, source_target_pairs={{4,0},{8,4},{12,8},{16,12},{20,16},{24,20},{28,24},{32,28},{36,32}... | collective-permute-start | bytes 3145736 | tf_op jit(solution)/shard_map/ppermute | solution.py:12
  231.9 68.4 %collective-permute-start.2 = (f32[128,512]{1,0:T(8,128)}, f32[128,512]{1,0:T(8,128)}, u32[]{:S(2)}, u32[]{:S(2)}) collective-permute-start(f32[128,512]{1,0:T(8,128)} %fusion.103), channel_id=1, source_target_pairs={{0,4},{4,8},{8,12},{12,16},{16,20},{20,24},{24,28},{28,32},{32,36}... | collective-permute-start | bytes 786440 | tf_op jit(solution)/shard_map/ppermute | solution.py:12
  293.7 4.2 copy-start.7
  303.4 16.8 %all-to-all-start.1 = ((f32[4,128,512]{1,2,0:T(8,128)}), f32[4,128,512]{1,2,0:T(8,128)S(1)}, u32[]{:S(2)}, u32[]{:S(2)}) async-start(f32[4,128,512]{1,2,0:T(8,128)} %stack.7), calls=%async_computation.1 | async-start | bytes 2097152 | tf_op jit(solution)/shard_map/all_to_all | solution.py:70
  306.9 149.9 %all-gather.8.cloned.1.call-start = ((), (), s32[]{:S(2)}) async-start(), calls=%async_computation.4 | async-start | bytes 1310720 | tf_op jit(solution)/shard_map/all_gather | solution.py:75
  453.7 29.5 %collective-permute-start.6 = (f32[512,512]{1,0:T(8,128)}, f32[512,512]{1,0:T(8,128)}, u32[]{:S(2)}, u32[]{:S(2)}) collective-permute-start(f32[512,512]{1,0:T(8,128)} %get-tuple-element.104), channel_id=1, source_target_pairs={{8,0},{12,4},{16,8},{20,12},{24,16},{28,20},{32,24},{36,28},{40,32... | collective-permute-start | bytes 3145736 | tf_op jit(solution)/shard_map/ppermute | solution.py:12
  462.1 84.0 %collective-permute-start.7 = (f32[512,512]{1,0:T(8,128)S(1)}, f32[512,512]{1,0:T(8,128)}, u32[]{:S(2)}, u32[]{:S(2)}) collective-permute-start(f32[512,512]{1,0:T(8,128)S(1)} %pad_maximum_fusion.2), channel_id=1, source_target_pairs={{8,0},{12,4},{16,8},{20,12},{24,16},{28,20},{32,24},{36,28},{40,32... | collective-permute-start | bytes 3145736 | tf_op jit(solution)/shard_map/ppermute | solution.py:12
  466.7 72.6 %collective-permute-start.5 = (f32[128,512]{1,0:T(8,128)}, f32[128,512]{1,0:T(8,128)}, u32[]{:S(2)}, u32[]{:S(2)}) collective-permute-start(f32[128,512]{1,0:T(8,128)} %fusion.101), channel_id=1, source_target_pairs={{0,8},{4,12},{8,16},{12,20},{16,24},{20,28},{24,32},{28,36},{32,40... | collective-permute-start | bytes 786440 | tf_op jit(solution)/shard_map/ppermute | solution.py:12
  532.6 4.2 copy-start.9
  542.3 18.4 %all-to-all-start.2 = ((f32[4,128,512]{1,2,0:T(8,128)}), f32[4,128,512]{1,2,0:T(8,128)S(1)}, u32[]{:S(2)}, u32[]{:S(2)}) async-start(f32[4,128,512]{1,2,0:T(8,128)} %stack.8), calls=%async_computation.2 | async-start | bytes 2097152 | tf_op jit(solution)/shard_map/all_to_all | solution.py:70
  545.9 198.6 %all-gather.10.cloned.1.call-start = ((), (), s32[]{:S(2)}) async-start(), calls=%async_computation.5 | async-start | bytes 1310720 | tf_op jit(solution)/shard_map/all_gather | solution.py:75
  647.0 49.9 %collective-permute-start.9 = (f32[512,512]{1,0:T(8,128)}, f32[512,512]{1,0:T(8,128)S(1)}, u32[]{:S(2)}, u32[]{:S(2)}) collective-permute-start(f32[512,512]{1,0:T(8,128)} %get-tuple-element.102), channel_id=1, source_target_pairs={{16,0},{20,4},{24,8},{28,12},{32,16},{36,20},{40,24},{44,28},{48,3... | collective-permute-start | bytes 3145736 | tf_op jit(solution)/shard_map/ppermute | solution.py:12
  697.0 49.4 %copy-start.8 = (f32[4,128,128]{1,2,0:T(8,128)S(1)}, f32[4,128,128]{1,2,0:T(8,128)}, u32[]{:S(2)}) copy-start(f32[4,128,128]{1,2,0:T(8,128)} %custom-call.47) | copy-start | bytes 786436
  750.6 49.8 %collective-permute-start.10 = (f32[512,512]{1,0:T(8,128)S(1)}, f32[512,512]{1,0:T(8,128)S(1)}, u32[]{:S(2)}, u32[]{:S(2)}) collective-permute-start(f32[512,512]{1,0:T(8,128)S(1)} %pad_maximum_fusion.4), channel_id=1, source_target_pairs={{16,0},{20,4},{24,8},{28,12},{32,16},{36,20},{40,24},{44,28},{48,3... | collective-permute-start | bytes 3145736 | tf_op jit(solution)/shard_map/ppermute | solution.py:12
  753.7 15.4 %collective-permute-start.8 = (f32[128,512]{1,0:T(8,128)S(1)}, f32[128,512]{1,0:T(8,128)S(1)}, u32[]{:S(2)}, u32[]{:S(2)}) collective-permute-start(f32[128,512]{1,0:T(8,128)S(1)} %fusion.99), channel_id=1, source_target_pairs={{0,16},{4,20},{8,24},{12,28},{16,32},{20,36},{24,40},{28,44},{32,4... | collective-permute-start | bytes 786440 | tf_op jit(solution)/shard_map/ppermute | solution.py:12
  (5 other events, 14.8 us)
Sparse Core Ops, SparseCore 0:
  21.9 42.0 all-gather.5
  74.5 30.3 all-gather.11
  310.4 27.9 all-gather.7
  549.1 28.7 all-gather.9
